TPU v7x, 128 devices: a whole 4x4x4 slice. The times are simulated.
128 devices in a mesh: span: 32 (over z, x, core), real: 4 (over y).
Axes of the slice: x: 4, y: 4, z: 4, core: 2. Of those that a mesh axis runs over, the one named last changes fastest.
Arguments:
- snapshots: float32 [8, 64, 512, 256], P('real', 'span'), may hold values from -10 to 10
- load: float32 [64, 512, 256], P('span'), may hold values from -6 to 6
- base_modulus: float32 [64, 512, 256], P('span'), may hold values from 0.5 to 2
- mistune: float32 [8], replicated, may hold values from 0.5 to 2
- material_ids: int32 [8, 32], replicated, may hold values from 0 to 7
- realization_map: int32 [8], P('real'), may hold values from 0 to 7, each once
- picks: int32 [2], replicated, may hold values from 0 to 7, as said below
Outputs:
- reduced_matrices: float32 [8, 2, 2], P('real')
- residual_fields: float32 [8, 64, 512, 256], P('real', 'span')
- residual_norms: float32 [8], P('real')
Inputs may be any that keep to these rules, and one draw needn't show every extreme that they name: `picks`: the two chosen snapshot indices differ, and one of them is the last snapshot, 7.
All inputs are finite; a program needn't handle non-finite values.
Results may differ from a plain program's by a relative error of at most 0.000075.
Values sent between devices are 32-bit elements; how exact they have to be, the bound alone decides.
A program may use at most 256 MiB of HBM per device.

v0:
```python
import jax
import jax.numpy as jnp
from jax import lax
from jax.sharding import PartitionSpec as P

NC = 512
SECTORS = 32


mass_shift = 0.5
self_weight = 14.0


def spread(value, axis, source):
    kept = jnp.where(lax.axis_index(axis) == source, value, 0).astype(value.dtype)
    return lax.psum(kept, axis)


def extended(cells, sides, width):
    for axis, dim in sides:
        count = lax.axis_size(axis)
        ends = count - 1
        head = lax.slice_in_dim(cells, 0, width, axis=dim)
        tail = lax.slice_in_dim(cells, cells.shape[dim] - width, cells.shape[dim], axis=dim)
        cells = jnp.concatenate(
            [
                lax.ppermute(tail, axis, [(i, (i + 1) % count) for i in range(ends)]),
                cells,
                lax.ppermute(head, axis, [((i + 1) % count, i) for i in range(ends)]),
            ],
            axis=dim,
        )
    return cells


def stencil_offsets():
    offsets = []
    for span_off in (-1, 0, 1):
        for circ_off in (-1, 0, 1):
            for axial_off in (-1, 0, 1):
                moved = abs(span_off) + abs(circ_off) + abs(axial_off)
                if moved > 0:
                    offsets.append((span_off, circ_off, axial_off, 1.0 / 2 ** (moved - 1)))
    return offsets


def neighbour_sum(padded):
    length = padded.shape[-3] - 2
    width = padded.shape[-1]
    widened = jnp.pad(padded, [(0, 0)] * (padded.ndim - 1) + [(1, 1)])
    weighted = jnp.zeros(padded.shape[:-3] + (length, padded.shape[-2], width), padded.dtype)
    for span_off, circ_off, axial_off, weight in stencil_offsets():
        shifted = widened[
            ..., 1 + span_off : 1 + span_off + length, :, 1 + axial_off : 1 + axial_off + width
        ]
        if circ_off != 0:
            shifted = jnp.roll(shifted, -circ_off, axis=-2)
        weighted = weighted + weight * shifted
    return weighted


def apply_stiffness(modulus, root_field, padded, basis):
    center = padded[..., 1:-1, :, :]
    return mass_shift * modulus * basis + root_field * (
        self_weight * center - neighbour_sum(padded)
    )


def circ_factors(material_ids, mistune, rows):
    chosen = jnp.take(material_ids, rows, axis=0)
    onehot = (
        chosen[:, :, None] == jnp.arange(mistune.shape[0], dtype=jnp.int32)[None, None, :]
    ).astype(jnp.float32)
    sector_factor = jnp.sum(onehot * mistune[None, None, :], axis=-1)
    return jnp.repeat(sector_factor, NC // SECTORS, axis=1)


def shards(snapshots, load, base_modulus, mistune, material_ids, realization_map, picks):
    cell_count = float(
        base_modulus.shape[0]
        * lax.axis_size("span")
        * base_modulus.shape[1]
        * base_modulus.shape[2]
    )
    held_count = snapshots.shape[0]

    def fetch(pick_index):
        owner_index = pick_index // held_count
        own_slab = lax.dynamic_index_in_dim(snapshots, pick_index % held_count, 0, keepdims=False)
        return spread(own_slab, "real", owner_index)

    first_slab = fetch(picks[0])
    norm_first = lax.psum(jnp.sum(first_slab * first_slab), "span") / cell_count
    basis_zero = first_slab / jnp.sqrt(norm_first)
    second_slab = fetch(picks[1])
    projected = lax.psum(jnp.sum(basis_zero * second_slab), "span") / cell_count
    remainder = second_slab - projected * basis_zero
    norm_second = lax.psum(jnp.sum(remainder * remainder), "span") / cell_count
    basis_one = remainder / jnp.sqrt(norm_second)
    factors = circ_factors(material_ids, mistune, realization_map)
    modulus = base_modulus[None] * factors[:, None, :, None]
    root_field = jnp.sqrt(modulus)
    bases = (basis_zero, basis_one)
    images = []
    column_list = []
    load_list = []
    for step_index in range(2):
        basis = bases[step_index]
        padded = extended(root_field * basis[None], (("span", 1),), 1)
        image_field = apply_stiffness(modulus, root_field, padded, basis[None])
        images.append(image_field)
        columns = jnp.stack(
            [
                jnp.sum(earlier[None] * image_field, axis=(1, 2, 3))
                for earlier in bases[: step_index + 1]
            ],
            axis=1,
        )
        load_proj = jnp.sum(bases[step_index] * load)
        columns, load_proj = lax.psum((columns, load_proj), "span")
        column_list.append(columns)
        load_list.append(load_proj)
    merged_columns = jnp.concatenate(column_list, axis=1)
    load_pair = jnp.stack(load_list)
    entry_aa = merged_columns[:, 0] / cell_count
    entry_ab = merged_columns[:, 1] / cell_count
    entry_bb = merged_columns[:, 2] / cell_count
    load_zero = load_pair[0] / cell_count
    load_one = load_pair[1] / cell_count
    determinant = entry_aa * entry_bb - entry_ab * entry_ab
    coeff_zero = (entry_bb * load_zero - entry_ab * load_one) / determinant
    coeff_one = (entry_aa * load_one - entry_ab * load_zero) / determinant
    residual_fields = (
        load[None]
        - coeff_zero[:, None, None, None] * images[0]
        - coeff_one[:, None, None, None] * images[1]
    )
    squared = lax.psum(jnp.sum(residual_fields * residual_fields, axis=(1, 2, 3)), "span")
    residual_norms = squared / cell_count
    reduced_matrices = jnp.stack(
        [jnp.stack([entry_aa, entry_ab], axis=1), jnp.stack([entry_ab, entry_bb], axis=1)], axis=1
    )
    return (reduced_matrices, residual_fields, residual_norms)


def solution(mesh):
    return jax.shard_map(
        shards,
        mesh=mesh,
        in_specs=(
            P("real", "span", None, None),
            P("span", None, None),
            P("span", None, None),
            P(),
            P(),
            P("real"),
            P(),
        ),
        out_specs=(P("real", None, None), P("real", "span", None, None), P("real")),
        check_vma=False,
    )
```

profile of v0, /device:TPU:1, one launch (start us, length us, event | category | flops | bytes accessed | tf_op | source)
XLA Modules:
  0.0 554.5 jit_solution(10776756867538176681)
XLA Ops:
  13.8 3.0 select_bitcast_fusion.1
  18.1 61.0 %all-reduce.6.cloned.1.call-done = (f32[2,512,256]{2,1,0:T(8,128)}, f32[2,512,256]{2,1,0:T(8,128)}) async-done(((f32[2,512,256]{2,1,0:T(8,128)}, f32[2,512,256]{2,1,0:T(8,128)}), (f32[2,512,256]{2,1,0:T(8,128)}, f32[2,512,256]{2,1,0:T(8,128)})) %all-reduce.6.cloned.1.call-update) | async-done | bytes 2097168 | tf_op jit(solution)/shard_map/psum | solution.py:16
  79.1 2.2 multiply_reduce_fusion.8
  81.3 63.5 %psum.71 = f32[]{:T(128)} all-reduce(f32[]{:T(128)} %multiply_reduce_fusion.8), channel_id=1, replica_groups=mesh['span'=32,'real'=4] {'span'}, use_global_device_ids=true, to_apply=%region_2.3 | all-reduce | flops 1 | bytes 8 | tf_op jit(solution)/shard_map/psum | solution.py:93
  145.5 2.5 broadcast_multiply_fusion.1
  148.9 67.7 %psum.74 = f32[]{:T(128)} all-reduce(f32[]{:T(128)} %multiply_reduce_fusion.7), channel_id=1, replica_groups=mesh['span'=32,'real'=4] {'span'}, use_global_device_ids=true, to_apply=%region_8.9 | all-reduce | flops 1 | bytes 8 | tf_op jit(solution)/shard_map/psum | solution.py:96
  218.3 63.3 %psum.75 = f32[]{:T(128)} all-reduce(f32[]{:T(128)} %multiply_reduce_fusion.6), channel_id=1, replica_groups=mesh['span'=32,'real'=4] {'span'}, use_global_device_ids=true, to_apply=%region_10.11 | all-reduce | flops 1 | bytes 8 | tf_op jit(solution)/shard_map/psum | solution.py:98
  284.5 1.9 collective-permute-start.2
  286.4 2.5 collective-permute-start.3
  290.4 3.1 collective-permute-start
  293.5 2.4 collective-permute-start.1
  298.1 4.4 collective-permute-done.3
  302.5 2.6 select_maximum_fusion
  305.1 2.7 copy-done.2
  307.9 21.1 %fusion.92 = (f32[2,2,511,256]{3,2,1,0:T(8,128)}, f32[2,2,511,256]{3,2,1,0:T(8,128)}, f32[2,2,511,256]{3,2,1,0:T(8,128)}, f32[2,2,511,256]{3,2,1,0:T(8,128)}, f3...) fusion(f32[2,4,512,258]{3,2,1,0:T(8,128)} %copy-done.2), kind=kLoop, calls=%fused_computation.198 | loop fusion | bytes 50233344 | tf_op jit(solution)/shard_map/jit(_roll_static)/slice | solution.py:57
  329.0 4.1 select_maximum_fusion.2
  333.2 2.6 copy-done.3
  336.0 20.9 %fusion.94 = (f32[2,2,511,256]{3,2,1,0:T(8,128)}, f32[2,2,511,256]{3,2,1,0:T(8,128)}, f32[2,2,511,256]{3,2,1,0:T(8,128)}, f32[2,2,511,256]{3,2,1,0:T(8,128)}, f3...) fusion(f32[2,4,512,258]{3,2,1,0:T(8,128)} %copy-done.3), kind=kLoop, calls=%fused_computation.200 | loop fusion | bytes 50233344 | tf_op jit(solution)/shard_map/jit(_roll_static)/slice | solution.py:57
  356.9 9.4 %fusion.44 = (f32[2,2,511,256]{3,2,1,0:T(8,128)}, f32[2,2,511,256]{3,2,1,0:T(8,128)}, f32[2,2,511,256]{3,2,1,0:T(8,128)}, f32[2,2,511,256]{3,2,1,0:T(8,128)}, f3...) fusion(f32[2,2,512,256]{3,2,1,0:T(8,128)} %copy-done.4, f32[2,1,512,256]{3,2,1,0:T(8,128)} %collective-permute-done, ...), kind=kLoop, calls=%fused_computation.78 | loop fusion | flops 2093056 | bytes 20946944 | tf_op jit(solution)/shard_map/concatenate | solution.py:25
  366.2 4.7 fusion.15
  370.9 44.0 %multiply_reduce_fusion.2 = (f32[2]{0:T(128)S(1)}, f32[2]{0:T(128)S(1)}, f32[2]{0:T(128)S(1)}, f32[2,2,512,256]{3,2,1,0:T(8,128)}, f32[2,2,512,256]{3,2,1,0:T(8,128)}) fusion(f32[2,512,256]{2,1,0:T(8,128)S(1)} %get-tuple-element.29, f32[2,512,256]{2,1,0:T(8,128)} %copy-done.5, f32[2,2,1,256]{3,2,1,0:T(1,128)S(1)} %get-tuple-element.65, ...), kind=kLoop, calls=%fused_computation.164 | loop fusion | flops 81264640 | bytes 118460440 | tf_op jit(solution)/shard_map/reduce_sum | solution.py:114
  414.9 57.6 %all-reduce.2 = (f32[2,2]{0,1:T(2,128)S(1)}, f32[2,1]{0,1:T(1,128)S(1)}, f32[]{:T(128)}, f32[]{:T(128)}) all-reduce(f32[2,2]{0,1:T(2,128)S(1)} %pad_maximum_fusion.9, f32[2,1]{0,1:T(1,128)S(1)} %bitcast.17, f32[]{:T(128)} %get-tuple-element.15, f32[]{:T(128)} %get-tuple-element.14), channel_id=1, replica_groups=mesh['span'=32,'real'=4] {'span'}, use_global_device_ids=true, to_apply=%region_13.14 | all-reduce | flops 8 | bytes 64 | tf_op jit(solution)/shard_map/psum | solution.py:120
  473.9 4.3 multiply_reduce_fusion
  478.2 68.2 %psum.79 = f32[2]{0:T(128)S(1)} all-reduce(f32[2]{0:T(128)S(1)} %get-tuple-element.23), channel_id=1, replica_groups=mesh['span'=32,'real'=4] {'span'}, use_global_device_ids=true, to_apply=%region_19.20 | all-reduce | flops 2 | bytes 16 | tf_op jit(solution)/shard_map/psum | solution.py:138
  (60 shorter events, 12.1 us)
Async XLA Ops:
  7.2 10.3 %copy-start = (s32[8,32]{1,0:T(8,128)S(1)}, s32[8,32]{1,0:T(8,128)}, u32[]{:S(2)}) copy-start(s32[8,32]{1,0:T(8,128)} %param.11) | copy-start | bytes 3076
  7.2 71.9 %all-reduce.6.cloned.1.call-start = ((), (), s32[]{:S(2)}) async-start(), calls=%async_computation | async-start | bytes 4194304 | tf_op jit(solution)/shard_map/psum | solution.py:16
  16.8 0.7 copy-start.14
  79.1 68.9 %copy-start.10 = (f32[2,512,256]{2,1,0:T(8,128)S(1)}, f32[2,512,256]{2,1,0:T(8,128)}, u32[]{:S(2)}) copy-start(f32[2,512,256]{2,1,0:T(8,128)} %get-tuple-element.21) | copy-start | bytes 3145732
  145.5 3.4 copy-start.13
  148.0 134.3 %copy-start.12 = (f32[2,512,256]{2,1,0:T(8,128)S(1)}, f32[2,512,256]{2,1,0:T(8,128)}, u32[]{:S(2)}) copy-start(f32[2,512,256]{2,1,0:T(8,128)} %param.8) | copy-start | bytes 3145732
  282.3 1.2 copy-start.11
  283.4 12.6 %copy-start.5 = (f32[2,512,256]{2,1,0:T(8,128)}, f32[2,512,256]{2,1,0:T(8,128)S(1)}, u32[]{:S(2)}) copy-start(f32[2,512,256]{2,1,0:T(8,128)S(1)} %get-tuple-element.25) | copy-start | bytes 3145732
  284.3 11.6 %copy-start.4 = (f32[2,2,512,256]{3,2,1,0:T(8,128)}, f32[2,2,512,256]{3,2,1,0:T(8,128)S(1)}, u32[]{:S(2)}) copy-start(f32[2,2,512,256]{3,2,1,0:T(8,128)S(1)} %get-tuple-element.105) | copy-start | bytes 6291460
  284.5 13.7 %collective-permute-start.2 = (f32[2,1,512,256]{3,2,1,0:T(8,128)S(1)}, f32[2,1,512,256]{3,2,1,0:T(8,128)S(1)}, u32[]{:S(2)}, u32[]{:S(2)}) collective-permute-start(f32[2,1,512,256]{3,2,1,0:T(8,128)S(1)} %get-tuple-element.92), channel_id=1, source_target_pairs={{0,4},{4,8},{8,12},{12,16},{16,20},{20,24},{24,28},{28,32},{32,36}... | collective-permute-start | bytes 3145736 | tf_op jit(solution)/shard_map/ppermute | solution.py:27
  286.4 16.1 %collective-permute-start.3 = (f32[2,1,512,256]{3,2,1,0:T(8,128)S(1)}, f32[2,1,512,256]{3,2,1,0:T(8,128)S(1)}, u32[]{:S(2)}, u32[]{:S(2)}) collective-permute-start(f32[2,1,512,256]{3,2,1,0:T(8,128)S(1)} %get-tuple-element.93), channel_id=1, source_target_pairs={{4,0},{8,4},{12,8},{16,12},{20,16},{24,20},{28,24},{32,28},{36,32}... | collective-permute-start | bytes 3145736 | tf_op jit(solution)/shard_map/ppermute | solution.py:29
  290.4 38.6 %collective-permute-start = (f32[2,1,512,256]{3,2,1,0:T(8,128)}, f32[2,1,512,256]{3,2,1,0:T(8,128)}, u32[]{:S(2)}, u32[]{:S(2)}) collective-permute-start(f32[2,1,512,256]{3,2,1,0:T(8,128)} %get-tuple-element.100), channel_id=1, source_target_pairs={{0,4},{4,8},{8,12},{12,16},{16,20},{20,24},{24,28},{28,32},{32,36}... | collective-permute-start | bytes 3145736 | tf_op jit(solution)/shard_map/ppermute | solution.py:27
  293.5 35.6 %collective-permute-start.1 = (f32[2,1,512,256]{3,2,1,0:T(8,128)}, f32[2,1,512,256]{3,2,1,0:T(8,128)}, u32[]{:S(2)}, u32[]{:S(2)}) collective-permute-start(f32[2,1,512,256]{3,2,1,0:T(8,128)} %get-tuple-element.101), channel_id=1, source_target_pairs={{4,0},{8,4},{12,8},{16,12},{20,16},{24,20},{28,24},{32,28},{36,32}... | collective-permute-start | bytes 3145736 | tf_op jit(solution)/shard_map/ppermute | solution.py:29
  298.1 7.0 %copy-start.6 = (f32[2,1,512,256]{3,2,1,0:T(8,128)}, f32[2,1,512,256]{3,2,1,0:T(8,128)S(1)}, u32[]{:S(2)}) copy-start(f32[2,1,512,256]{3,2,1,0:T(8,128)S(1)} %collective-permute-done.2) | copy-start | bytes 3145732
  302.5 2.6 copy-start.8
  305.1 2.7 copy-start.2
  333.2 2.7 copy-start.3
  356.8 9.4 %copy-start.7 = (f32[2,1,512,256]{3,2,1,0:T(8,128)S(1)}, f32[2,1,512,256]{3,2,1,0:T(8,128)}, u32[]{:S(2)}) copy-start(f32[2,1,512,256]{3,2,1,0:T(8,128)} %copy-done.6) | copy-start | bytes 3145732
  356.8 9.4 %copy-start.9 = (f32[2,1,512,256]{3,2,1,0:T(8,128)S(1)}, f32[2,1,512,256]{3,2,1,0:T(8,128)}, u32[]{:S(2)}) copy-start(f32[2,1,512,256]{3,2,1,0:T(8,128)} %copy-done.8) | copy-start | bytes 3145732
  473.9 73.8 %copy-start.1 = (s32[8,32]{1,0:T(8,128)S(1)}, s32[8,32]{1,0:T(8,128)}, u32[]{:S(2)}) copy-start(s32[8,32]{1,0:T(8,128)} %param.11) | copy-start | bytes 3076
Sparse Core Ops, SparseCore 0:
  17.0 62.0 all-reduce.5
where the time goes:
time: 555 us
  blocking collectives  320 us (58%)
  other arithmetic  82 us (15%)
  waiting for transfers between devices  66.6 us (12%)
  local copies, waits for them, and re-layouts  52.9 us (10%)
  between operations  22.9 us (4%)
  starting transfers between devices  9.91 us (2%)
    psum x1, blocking collectives, shards(): lax.psum(jnp.sum(residual_fields * residual_fields, axis=(1, 2, 3)), 'span')  68.2 us
    psum x1, blocking collectives, shards(): projected = lax.psum(jnp.sum(basis_zero * second_slab), 'span') / cell_count  67.7 us
    psum x1, blocking collectives, shards(): norm_first = lax.psum(jnp.sum(first_slab * first_slab), 'span') / cell_count  63.5 us
    psum x1, blocking collectives, shards(): norm_second = lax.psum(jnp.sum(remainder * remainder), 'span') / cell_count  63.3 us
    psum x1, waiting for transfers between devices, spread(): return lax.psum(kept, axis)  61 us
    psum x1, blocking collectives, shards(): columns, load_proj = lax.psum((columns, load_proj), 'span')  57.6 us
    reduce_sum x1, other arithmetic, shards(): jnp.sum(earlier[None] * image_field, axis=(1, 2, 3))  44 us
    slice x5, local copies, waits for them, and re-layouts, neighbour_sum(): shifted = jnp.roll(shifted, -circ_off, axis=-2)  42.2 us
  transfers between devices with their start and end apart: 5, of which 3 were waited for; matrix products, arithmetic and copies ran while one was open for 5% of the time, Pallas kernels for 0%

commit v1 on v0

v1 whole, which is shorter than its diff:
```python
import functools

import jax
import jax.numpy as jnp
from jax import lax
from jax.experimental import pallas as pl
from jax.experimental.pallas import tpu as pltpu
from jax.sharding import PartitionSpec as P

MESH = pl.DeviceIdType.MESH
SHIFT = 0.5
ROWS = 32
LAG = 1
PAD = 8
LANES = 128
F32 = jnp.float32


def kernel(
    owner, picks, mistune, ids, slots, snaps, load_in, base_in,
    red, res, nrm,
    field, edge, both, load, root, root_edge, mixed, image, factor, pair, totals, near, far,
    local_sem, send_sem, recv_sem, edge_send, edge_recv, root_send, root_recv,
    near_send, near_recv, far_send, far_recv,
):
    n_span, n_real = lax.axis_size("span"), lax.axis_size("real")
    span, real = lax.axis_index("span"), lax.axis_index("real")
    held, planes, circ, axial = snaps.shape
    sectors = ids.shape[1]
    width = circ // sectors
    pieces = circ // ROWS
    last = held * n_real - 1
    owners = (owner, n_real - 1)
    cells = float(planes * n_span * circ * axial)
    n_near, n_far = near.shape[0], far.shape[0]

    before, after = lax.rem(span + n_span - 1, n_span), lax.rem(span + 1, n_span)
    below, above = lax.rem(real + n_real - 1, n_real), lax.rem(real + 1, n_real)
    my_far, my_near = lax.div(span, n_near), lax.rem(span, n_near)

    def near_peer(i):
        return my_far * n_near + lax.rem(my_near + i, n_near)

    def far_peer(i):
        return lax.rem(my_far + i, n_far) * n_near + my_near

    barrier = pltpu.get_barrier_semaphore()
    greeted = 0
    for where in [{"real": below}, {"real": above}, {"span": before}, {"span": after}]:
        pl.semaphore_signal(barrier, inc=1, device_id=where, device_id_type=MESH)
        greeted += 1
    for i in range(1, n_near):
        pl.semaphore_signal(barrier, inc=1, device_id={"span": near_peer(i)}, device_id_type=MESH)
        greeted += 1
    for i in range(1, n_far):
        pl.semaphore_signal(barrier, inc=1, device_id={"span": far_peer(i)}, device_id_type=MESH)
        greeted += 1

    base_copy = pltpu.make_async_copy(base_in, root, local_sem.at[0])
    load_copy = pltpu.make_async_copy(load_in, load, local_sem.at[1])
    last_copy = pltpu.make_async_copy(snaps.at[held - 1], field.at[1], local_sem.at[2])
    if owner == n_real - 1:
        other_copy = pltpu.make_async_copy(snaps.at[0], field.at[0], local_sem.at[3])
    else:
        other_copy = pltpu.make_async_copy(snaps, both, local_sem.at[3])

    @pl.when(real == owner)
    def _():
        other_copy.start()

    @pl.when(real == n_real - 1)
    def _():
        last_copy.start()

    base_copy.start()
    load_copy.start()

    def fill(j, carry):
        for t in range(2):
            value = mistune[ids[slots[t], j]]
            factor[t, pl.ds(PAD + j * width, width), :] = jnp.full((width, LANES), value, F32)
        return carry

    lax.fori_loop(0, sectors, fill, 0)
    for t in range(2):
        factor[t, 0:PAD, :] = factor[t, circ : circ + PAD, :]
        factor[t, circ + PAD : circ + 2 * PAD, :] = factor[t, PAD : 2 * PAD, :]
        here = factor[t, PAD : circ + PAD, :]
        for side, shift in ((0, -1), (1, 1)):
            pair[t, side] = jnp.sqrt(here * factor[t, PAD + shift : circ + PAD + shift, :])
    totals[...] = jnp.zeros_like(totals)

    @pl.when(real == owner)
    def _():
        other_copy.wait()
        if owner != n_real - 1:
            chosen = lax.rem(jnp.minimum(picks[0], picks[1]), held)

            def choose(i, carry):
                rows = pl.ds(pl.multiple_of(i * 16, 16), 16)
                for p in range(planes):
                    field[0, p, rows, :] = jnp.where(chosen == 0, both[0, p, rows, :], both[1, p, rows, :])
                return carry

            lax.fori_loop(0, circ // 16, choose, 0)

    @pl.when(real == n_real - 1)
    def _():
        last_copy.wait()

    base_copy.wait()

    def take_root(i, carry):
        rows = pl.ds(pl.multiple_of(i * 16, 16), 16)
        for p in range(planes):
            root[p, rows, :] = jnp.sqrt(root[p, rows, :])
        return carry

    lax.fori_loop(0, circ // 16, take_root, 0)
    pl.semaphore_wait(barrier, greeted)

    def root_hop(p):
        return pltpu.make_async_remote_copy(
            src_ref=root.at[p],
            dst_ref=root_edge.at[1 - p],
            send_sem=root_send.at[p],
            recv_sem=root_recv.at[1 - p],
            device_id={"span": before if p == 0 else after},
            device_id_type=MESH,
        )

    for p in range(2):
        root_hop(p).start()

    def rows_of(k):
        return pl.ds(pl.multiple_of(k * ROWS, ROWS), ROWS)

    def hop(s, p, k):
        return pltpu.make_async_remote_copy(
            src_ref=field.at[s, p, rows_of(k)],
            dst_ref=field.at[s, p, rows_of(k)],
            send_sem=send_sem.at[s, p],
            recv_sem=recv_sem.at[s, p, k],
            device_id={"real": above if p == 0 else below},
            device_id_type=MESH,
        )

    def edge_hop(s, p, k):
        return pltpu.make_async_remote_copy(
            src_ref=field.at[s, p, rows_of(k)],
            dst_ref=edge.at[s, 1 - p, rows_of(k)],
            send_sem=edge_send.at[s, p],
            recv_sem=edge_recv.at[s, 1 - p, k],
            device_id={"span": before if p == 0 else after},
            device_id_type=MESH,
        )

    distance = [
        (lax.rem(real + n_real - owners[s], n_real), lax.rem(owners[s] + n_real - real, n_real)) for s in range(2)
    ]

    low = jnp.where(span > 0, 0.5, 0.0).astype(F32)
    high = jnp.where(span < n_span - 1, 0.5, 0.0).astype(F32)
    column = lax.broadcasted_iota(jnp.int32, (8, axial), 1)
    not_first, not_last = column > 0, column < axial - 1

    def mix(k, carry):
        start = pl.multiple_of(k * 8, 8)
        rows = pl.ds(start, 8)
        q0, q1, ql, qh = root[0, rows, :], root[1, rows, :], root_edge[0, rows, :], root_edge[1, rows, :]
        for s in range(2):
            w0, w1 = q0 * field[s, 0, rows, :], q1 * field[s, 1, rows, :]
            wl, wh = ql * edge[s, 0, rows, :], qh * edge[s, 1, rows, :]
            for p, across in ((0, w0 + (low * wl + 0.5 * w1)), (1, w1 + (high * wh + 0.5 * w0))):
                left = jnp.where(not_first, pltpu.roll(across, 1, 1), 0.0)
                right = jnp.where(not_last, pltpu.roll(across, axial - 1, 1), 0.0)
                mixed[s, p, pl.ds(start + PAD, 8), :] = across + 0.5 * (left + right)
        return carry

    def fold(x):
        return x[:, :LANES] + x[:, LANES:]

    def work(j, carry):
        parts = [None] * 22

        def add(i, x):
            x = fold(x)
            parts[i] = x if parts[i] is None else parts[i] + x

        for h in range(width // 8):
            start = pl.multiple_of(j * width + h * 8, 8)
            rows = pl.ds(start, 8)
            wide = lambda x: jnp.concatenate([x] * (axial // LANES), axis=1)
            fac = [wide(factor[t, pl.ds(start + PAD, 8), :]) for t in range(2)]
            prev = [wide(pair[t, 0, rows, :]) for t in range(2)]
            succ = [wide(pair[t, 1, rows, :]) for t in range(2)]
            for p in range(planes):
                q, force = root[p, rows, :], load[p, rows, :]
                x0, x1 = field[0, p, rows, :], field[1, p, rows, :]
                images = [[None, None], [None, None]]
                for s, x in ((0, x0), (1, x1)):
                    tall = mixed[s, p, pl.ds(start + PAD - 8, 24), :]
                    up, centre, down = tall[7:15], tall[8:16], tall[9:17]
                    inner = (16.0 + SHIFT) * (q * x) - 2.0 * centre
                    for t in range(2):
                        im = q * (fac[t] * inner - (prev[t] * up + succ[t] * down))
                        image[t, s, p, rows, :] = im
                        images[t][s] = im
                for t in range(2):
                    i0, i1 = images[t]
                    add(8 * t + 0, x0 * i0)
                    add(8 * t + 1, x0 * i1)
                    add(8 * t + 2, x1 * i1)
                    add(8 * t + 3, force * i0)
                    add(8 * t + 4, force * i1)
                    add(8 * t + 5, i0 * i0)
                    add(8 * t + 6, i0 * i1)
                    add(8 * t + 7, i1 * i1)
                add(16, x0 * x0)
                add(17, x0 * x1)
                add(18, x1 * x1)
                add(19, force * x0)
                add(20, force * x1)
                add(21, force * force)
        for i in range(22):
            totals[i] += parts[i]
        return carry

    def step(tau, carry):
        for s in (1, 0):
            for p in range(2):
                far_off = distance[s][p]
                k = tau - far_off

                @pl.when((k >= 0) & (k < pieces))
                def _():
                    @pl.when(far_off > 0)
                    def _():
                        hop(s, p, k).wait_recv()

                    @pl.when(far_off < n_real - 1)
                    def _():
                        hop(s, p, k).start()

                    edge_hop(s, p, k).start()

        done = tau - (n_real - 1) - LAG

        @pl.when(done == 0)
        def _():
            load_copy.wait()
            for p in range(2):
                root_hop(p).wait_recv()

        @pl.when(done >= 0)
        def _():
            for s in range(2):
                for p in range(2):
                    edge_hop(s, p, done).wait_recv()
            lax.fori_loop(done * (ROWS // 8), (done + 1) * (ROWS // 8), mix, 0)
            per = ROWS // width
            lax.fori_loop(jnp.maximum(done * per - 1, 1), (done + 1) * per - 1, work, 0)

        return carry

    lax.fori_loop(0, pieces + n_real - 1 + LAG, step, 0)

    for s in range(2):
        for p in range(2):
            mixed[s, p, 0:PAD, :] = mixed[s, p, circ : circ + PAD, :]
            mixed[s, p, circ + PAD : circ + 2 * PAD, :] = mixed[s, p, PAD : 2 * PAD, :]
    lax.fori_loop(0, 2, lambda i, c: work((1 - i) * (sectors - 1), c), 0)

    lane = lax.broadcasted_iota(jnp.int32, (8, LANES), 1)
    packed = jnp.zeros((8, LANES), F32)
    for g in range(3):
        v = jnp.sum(totals[8 * g : 8 * g + 8], axis=1)
        v = v + pltpu.roll(v, 64, 1)
        v = v + pltpu.roll(v, 32, 1)
        packed = jnp.where((lane >= 32 * g) & (lane < 32 * g + 32), v, packed)

    def near_hop(i):
        return pltpu.make_async_remote_copy(
            src_ref=near.at[my_near],
            dst_ref=near.at[my_near],
            send_sem=near_send.at[i],
            recv_sem=near_recv.at[i],
            device_id={"span": near_peer(i)},
            device_id_type=MESH,
        )

    def far_hop(i):
        return pltpu.make_async_remote_copy(
            src_ref=far.at[my_far],
            dst_ref=far.at[my_far],
            send_sem=far_send.at[i],
            recv_sem=far_recv.at[i],
            device_id={"span": far_peer(i)},
            device_id_type=MESH,
        )

    near[my_near] = packed
    for i in range(1, n_near):
        near_hop(i).start()
    for i in range(1, n_near):
        near_hop(i).wait_recv()
    far[my_far] = jnp.sum(near[...], axis=0)
    for i in range(1, n_far):
        far_hop(i).start()
    for i in range(1, n_far):
        far_hop(i).wait_recv()

    group = lax.broadcasted_iota(jnp.int32, (1, LANES), 1) // 32
    rows = [far[:, r, :] for r in range(8)]

    def one(x, g):
        return jnp.sum(jnp.where(group == g, x, 0.0), axis=1, keepdims=True)

    def total(x):
        x = jnp.sum(x, axis=0, keepdims=True)
        return jnp.where(group == 0, one(x, 0), one(x, 1)) / cells

    def shared(x):
        return one(jnp.sum(x, axis=0, keepdims=True), 2) / cells

    swapped = picks[0] == last
    r00, r01, r11 = jnp.where(swapped, rows[2], rows[0]), rows[1], jnp.where(swapped, rows[0], rows[2])
    f0, f1 = jnp.where(swapped, rows[4], rows[3]), jnp.where(swapped, rows[3], rows[4])
    norm0 = shared(r00)
    along = shared(r01) / norm0
    rest = r11 - 2.0 * along * r01 + along * along * r00
    norm1 = shared(rest)
    inv0, inv1 = 1.0 / jnp.sqrt(norm0), 1.0 / jnp.sqrt(norm1)
    a00 = total(r00) * inv0 * inv0
    a01 = total(r01 - along * r00) * inv0 * inv1
    a11 = total(rest) * inv1 * inv1
    b0, b1 = shared(f0) * inv0, shared(f1 - along * f0) * inv1
    det = a00 * a11 - a01 * a01
    c0, c1 = (a11 * b0 - a01 * b1) / det, (a00 * b1 - a01 * b0) / det
    second = c1 * inv1
    first = c0 * inv0 - along * second
    g0, g1 = jnp.where(swapped, second, first), jnp.where(swapped, first, second)
    power = jnp.where(group == 0, pltpu.roll(rows[5], 64, 1), pltpu.roll(rows[5], 96, 1))
    square = total(
        power
        - 2.0 * (g0 * rows[3] + g1 * rows[4])
        + (g0 * g0 * rows[5] + 2.0 * g0 * g1 * rows[6] + g1 * g1 * rows[7])
    )
    spot = lax.broadcasted_iota(jnp.int32, (1, LANES), 1)

    def scalar(x, t):
        return jnp.sum(jnp.where(spot == 32 * t, x, 0.0))

    for t in range(2):
        red[t, 0, 0] = scalar(a00, t)
        red[t, 0, 1] = scalar(a01, t)
        red[t, 1, 0] = scalar(a01, t)
        red[t, 1, 1] = scalar(a11, t)
        nrm[t] = scalar(square, t)

    scale = [[jnp.sum(jnp.where(spot == 32 * t, g, 0.0), axis=1, keepdims=True) for g in (g0, g1)] for t in range(2)]
    blocks = 8
    tall = circ // blocks

    def out_copy(t, b):
        rows = pl.ds(pl.multiple_of(b * tall, tall), tall)
        return pltpu.make_async_copy(image.at[t, 0, :, rows], res.at[t, :, rows], local_sem.at[4 + t])

    def finish(b, carry):
        def block(i, c):
            rows = pl.ds(pl.multiple_of(b * tall + i * 8, 8), 8)
            for p in range(planes):
                force = load[p, rows, :]
                for t in range(2):
                    image[t, 0, p, rows, :] = force - (
                        scale[t][0] * image[t, 0, p, rows, :] + scale[t][1] * image[t, 1, p, rows, :]
                    )
            return c

        lax.fori_loop(0, tall // 8, block, 0)
        for t in range(2):
            out_copy(t, b).start()
        return carry

    lax.fori_loop(0, blocks, finish, 0)

    for p in range(2):
        root_hop(p).wait_send()
    for i in range(1, n_near):
        near_hop(i).wait_send()
    for i in range(1, n_far):
        far_hop(i).wait_send()

    def whole(s, p, sem):
        return pltpu.make_async_copy(field.at[s, p], field.at[s, p], sem)

    for s in range(2):
        for p in range(2):
            whole(s, p, edge_send.at[s, p]).wait()

            @pl.when(distance[s][p] < n_real - 1)
            def _():
                whole(s, p, send_sem.at[s, p]).wait()

    for t in range(2):
        pltpu.make_async_copy(image.at[t, 0], res.at[t], local_sem.at[4 + t]).wait()


def shards(snapshots, load, base_modulus, mistune, material_ids, realization_map, picks):
    n_span, n_real = lax.axis_size("span"), lax.axis_size("real")
    held, planes, circ, axial = snapshots.shape
    n_near = 8 if n_span % 8 == 0 else 2
    n_far = n_span // n_near
    pieces = circ // ROWS
    vmem = lambda *shape: pltpu.VMEM(shape, F32)
    dma = lambda *shape: pltpu.SemaphoreType.DMA(shape)

    def run(owner):
        return pl.pallas_call(
            functools.partial(kernel, owner),
            out_shape=(
                jax.ShapeDtypeStruct((2, 2, 2), F32),
                jax.ShapeDtypeStruct((2, planes, circ, axial), F32),
                jax.ShapeDtypeStruct((2,), F32),
            ),
            in_specs=[pl.BlockSpec(memory_space=pltpu.SMEM)] * 4 + [pl.BlockSpec(memory_space=pl.ANY)] * 3,
            out_specs=(
                pl.BlockSpec(memory_space=pltpu.SMEM),
                pl.BlockSpec(memory_space=pl.ANY),
                pl.BlockSpec(memory_space=pltpu.SMEM),
            ),
            scratch_shapes=[
                vmem(2, planes, circ, axial),
                vmem(2, 2, circ, axial),
                vmem(held, planes, circ, axial),
                vmem(planes, circ, axial),
                vmem(planes, circ, axial),
                vmem(2, circ, axial),
                vmem(2, planes, circ + 2 * PAD, axial),
                vmem(2, 2, planes, circ, axial),
                vmem(2, circ + 2 * PAD, LANES),
                vmem(2, 2, circ, LANES),
                vmem(24, 8, LANES),
                vmem(n_near, 8, LANES),
                vmem(n_far, 8, LANES),
                dma(6),
                dma(2, 2),
                dma(2, 2, pieces),
                dma(2, 2),
                dma(2, 2, pieces),
                dma(2),
                dma(2),
                dma(n_near),
                dma(n_near),
                dma(n_far),
                dma(n_far),
            ],
            compiler_params=pltpu.CompilerParams(
                collective_id=owner, has_side_effects=True, vmem_limit_bytes=40 * 2**20
            ),
        )(picks, mistune, material_ids, realization_map, snapshots, load, base_modulus)

    other = jnp.minimum(picks[0], picks[1])
    return lax.switch(
        lax.div(other, jnp.int32(held)), [lambda owner=owner: run(owner) for owner in range(n_real)]
    )


def solution(mesh):
    return jax.shard_map(
        shards,
        mesh=mesh,
        in_specs=(
            P("real", "span", None, None),
            P("span", None, None),
            P("span", None, None),
            P(),
            P(),
            P("real"),
            P(),
        ),
        out_specs=(P("real", None, None), P("real", "span", None, None), P("real")),
        check_vma=False,
    )
```

time: 555 us -> 83.5 us (0.15)
  blocking collectives: 320 us -> 0 us
  other arithmetic: 82 us -> 0 us
  Pallas kernels: 0 us -> 77.6 us
  waiting for transfers between devices: 66.6 us -> 0 us
  local copies, waits for them, and re-layouts: 52.9 us -> 3.72 us
  between operations: 22.9 us -> 1.95 us
  starting transfers between devices: 9.91 us -> 0 us
    psum x5 -> x0, blocking collectives: 320 us -> none  [the longest x1 68.2 us: shards(): lax.psum(jnp.sum(residual_fields * residual_fields, axis=(1, 2, 3)), 'span')]
    pallas_call x0 -> x1, Pallas kernels: none -> 77.6 us  [run(): pl.pallas_call(functools.partial(kernel, owner), out_shape=(jax.ShapeDtyp...]
    psum x1 -> x0, waiting for transfers between devices: 61 us -> none  [spread(): return lax.psum(kept, axis)]
    reduce_sum x7 -> x0, other arithmetic: 53.4 us -> none  [the longest x1 44 us: shards(): jnp.sum(earlier[None] * image_field, axis=(1, 2, 3))]
    slice x8 -> x1, local copies, waits for them, and re-layouts: 45.2 us -> 1.31 us  [shards(): other = jnp.minimum(picks[0], picks[1])]
    concatenate x4 -> x0, other arithmetic: 20.8 us -> none  [extended(): jnp.concatenate([lax.ppermute(tail, axis, [(i, (i + 1) % count) for i in...]
    ppermute x4 -> x0, starting transfers between devices: 9.87 us -> none  [the longest x2 5 us: extended(): lax.ppermute(tail, axis, [(i, (i + 1) % count) for i in range(ends)])]
  transfers between devices with their start and end apart: 5 -> 0, of which waited for: 3 -> 0; matrix products, arithmetic and copies ran while one was open for 5% -> 0% of each run, Pallas kernels for 0% -> 0%
where the time goes in v1:
time: 83.5 us; the launch traced here: 83.3 us
  Pallas kernels  77.6 us (93%)
  local copies, waits for them, and re-layouts  3.72 us (4%)
  between operations  1.95 us (2%)
    pallas_call x1, Pallas kernels, run(): pl.pallas_call(functools.partial(kernel, owner), out_shape=(jax.ShapeDtyp...  77.6 us
    unnamed x3, local copies, waits for them, and re-layouts  2.41 us

profile of v1, /device:TPU:1, one launch (start us, length us, event | category | flops | bytes accessed | tf_op | source)
XLA Modules:
  0.0 83.3 jit_solution(7901021451555026810)
XLA Ops:
  0.6 1.3 %fusion = (s32[1]{0:T(128)}, s32[1]{0:T(128)}) fusion(s32[2]{0:T(128)} %param.17), kind=kLoop, calls=%fused_computation | loop fusion | bytes 16 | tf_op jit(solution)/shard_map/slice | solution.py:463
  3.3 77.6 %conditional.1 = ((f32[2,2,2]{2,1,0:T(2,128)S(1)}, f32[2,2,512,256]{3,2,1,0:T(8,128)S(1)}, f32[2]{0:T(128)S(1)})) conditional(s32[]{:T(128)} %clamp.3, (s32[2]{0:T(128)}, f32[8]{0:T(128)}, s32[8,32]{1,0:T(8,128)}, s32[2]{0:T(128)}, f32[2,2,512,256]{3,2,1,0:T(8,128)}, /*index=5*/f32[2,512,256]{2,1,0:T(8,128)}, ...), branch_computations={%region_0.0_spmd, %region_1.0_spmd, %region_2.0_spmd, %region_3.0_... | conditional | bytes 8 | solution.py:464
  3.3 77.6 %branch_1_fun.1 = (f32[2,2,2]{2,1,0:T(2,128)S(1)}, f32[2,2,512,256]{3,2,1,0:T(8,128)S(1)}, f32[2]{0:T(128)S(1)}) custom-call(s32[2]{0:T(128)} %get-tuple-element.63.picks, f32[8]{0:T(128)} %get-tuple-element.64.mistune, s32[8,32]{1,0:T(8,128)} %get-tuple-element.65.ids, s32[2]{0:T(128)} %get-tuple-element.66.slots, ...), custom_call_target="tpu_custom_call" | custom-call | tf_op jit(solution)/shard_map/cond/branch_1_fun/pallas_call | solution.py:419
  80.9 0.6 copy.37
  81.4 1.3 %copy.38 = f32[2,2,512,256]{3,2,1,0:T(8,128)} copy(f32[2,2,512,256]{3,2,1,0:T(8,128)S(1)} %get-tuple-element.120) | data formatting | bytes 4194304
  82.8 0.5 copy.39

commit v2 on v1

--- a/solution.py
+++ b/solution.py
@@ -10,28 +10,29 @@
 MESH = pl.DeviceIdType.MESH
 SHIFT = 0.5
 ROWS = 32
-LAG = 1
+DEPTH = 2
+LAG = 2
 PAD = 8
 LANES = 128
 F32 = jnp.float32
 
 
-def kernel(
-    owner, picks, mistune, ids, slots, snaps, load_in, base_in,
-    red, res, nrm,
-    field, edge, both, load, root, root_edge, mixed, image, factor, pair, totals, near, far,
-    local_sem, send_sem, recv_sem, edge_send, edge_recv, root_send, root_recv,
+def gather_kernel(
+    picks_in, mistune_in, ids_in, slots_in, snaps, load_in, base_in,
+    image, load, far, order,
+    picks, mistune, ids, slots,
+    field, edge, both, own, sent, got, root, root_edge, mixed, factor, pair, totals, near,
+    small_sem, local_sem, send_sem, recv_sem, sent_sem, got_sem, edge_send, edge_recv, root_send, root_recv,
     near_send, near_recv, far_send, far_recv,
 ):
     n_span, n_real = lax.axis_size("span"), lax.axis_size("real")
     span, real = lax.axis_index("span"), lax.axis_index("real")
     held, planes, circ, axial = snaps.shape
-    sectors = ids.shape[1]
+    sectors = ids_in.shape[1]
     width = circ // sectors
     pieces = circ // ROWS
     last = held * n_real - 1
-    owners = (owner, n_real - 1)
-    cells = float(planes * n_span * circ * axial)
+    slots_sent = pieces + (n_real - 2) * DEPTH
     n_near, n_far = near.shape[0], far.shape[0]
 
     before, after = lax.rem(span + n_span - 1, n_span), lax.rem(span + 1, n_span)
@@ -56,24 +57,28 @@
         pl.semaphore_signal(barrier, inc=1, device_id={"span": far_peer(i)}, device_id_type=MESH)
         greeted += 1
 
+    smalls = [
+        pltpu.make_async_copy(src, dst, small_sem.at[i])
+        for i, (src, dst) in enumerate(((picks_in, picks), (mistune_in, mistune), (ids_in, ids), (slots_in, slots)))
+    ]
     base_copy = pltpu.make_async_copy(base_in, root, local_sem.at[0])
     load_copy = pltpu.make_async_copy(load_in, load, local_sem.at[1])
     last_copy = pltpu.make_async_copy(snaps.at[held - 1], field.at[1], local_sem.at[2])
-    if owner == n_real - 1:
-        other_copy = pltpu.make_async_copy(snaps.at[0], field.at[0], local_sem.at[3])
-    else:
-        other_copy = pltpu.make_async_copy(snaps, both, local_sem.at[3])
-
-    @pl.when(real == owner)
-    def _():
-        other_copy.start()
+    both_copy = pltpu.make_async_copy(snaps, both, local_sem.at[3])
+    for copy in smalls:
+        copy.start()
+    base_copy.start()
+    both_copy.start()
 
     @pl.when(real == n_real - 1)
     def _():
         last_copy.start()
 
-    base_copy.start()
     load_copy.start()
+    for copy in smalls:
+        copy.wait()
+    other = jnp.minimum(picks[0], picks[1])
+    order[...] = jnp.full(order.shape, jnp.where(picks[0] == last, 1.0, 0.0), F32)
 
     def fill(j, carry):
         for t in range(2):
@@ -90,33 +95,23 @@
             pair[t, side] = jnp.sqrt(here * factor[t, PAD + shift : circ + PAD + shift, :])
     totals[...] = jnp.zeros_like(totals)
 
-    @pl.when(real == owner)
-    def _():
-        other_copy.wait()
-        if owner != n_real - 1:
-            chosen = lax.rem(jnp.minimum(picks[0], picks[1]), held)
-
-            def choose(i, carry):
-                rows = pl.ds(pl.multiple_of(i * 16, 16), 16)
-                for p in range(planes):
-                    field[0, p, rows, :] = jnp.where(chosen == 0, both[0, p, rows, :], both[1, p, rows, :])
-                return carry
-
-            lax.fori_loop(0, circ // 16, choose, 0)
-
-    @pl.when(real == n_real - 1)
-    def _():
-        last_copy.wait()
-
     base_copy.wait()
+    both_copy.wait()
+    chosen = lax.rem(other, held)
 
     def take_root(i, carry):
         rows = pl.ds(pl.multiple_of(i * 16, 16), 16)
         for p in range(planes):
             root[p, rows, :] = jnp.sqrt(root[p, rows, :])
+            own[p, rows, :] = jnp.where(chosen == 0, both[0, p, rows, :], both[held - 1, p, rows, :])
         return carry
 
     lax.fori_loop(0, circ // 16, take_root, 0)
+
+    @pl.when(real == n_real - 1)
+    def _():
+        last_copy.wait()
+
     pl.semaphore_wait(barrier, greeted)
 
     def root_hop(p):
@@ -135,13 +130,26 @@
     def rows_of(k):
         return pl.ds(pl.multiple_of(k * ROWS, ROWS), ROWS)
 
-    def hop(s, p, k):
+    def along(p):
+        return {"real": above if p == 0 else below}
+
+    def hop(p, k):
         return pltpu.make_async_remote_copy(
-            src_ref=field.at[s, p, rows_of(k)],
-            dst_ref=field.at[s, p, rows_of(k)],
-            send_sem=send_sem.at[s, p],
-            recv_sem=recv_sem.at[s, p, k],
-            device_id={"real": above if p == 0 else below},
+            src_ref=field.at[1, p, rows_of(k)],
+            dst_ref=field.at[1, p, rows_of(k)],
+            send_sem=send_sem.at[p],
+            recv_sem=recv_sem.at[p, k],
+            device_id=along(p),
+            device_id_type=MESH,
+        )
+
+    def pass_on(p, k):
+        return pltpu.make_async_remote_copy(
+            src_ref=sent.at[p, rows_of(k)],
+            dst_ref=got.at[p, rows_of(k)],
+            send_sem=sent_sem.at[p],
+            recv_sem=got_sem.at[p, k],
+            device_id=along(p),
             device_id_type=MESH,
         )
 
@@ -155,9 +163,9 @@
             device_id_type=MESH,
         )
 
-    distance = [
-        (lax.rem(real + n_real - owners[s], n_real), lax.rem(owners[s] + n_real - real, n_real)) for s in range(2)
-    ]
+    distance = (real + 1) % n_real, n_real - 1 - real
+    owner = lax.div(other, held)
+    from_owner = (lax.rem(real + n_real - owner, n_real), lax.rem(owner + n_real - real, n_real))
 
     low = jnp.where(span > 0, 0.5, 0.0).astype(F32)
     high = jnp.where(span < n_span - 1, 0.5, 0.0).astype(F32)
@@ -227,24 +235,50 @@
         return carry
 
     def step(tau, carry):
-        for s in (1, 0):
-            for p in range(2):
-                far_off = distance[s][p]
-                k = tau - far_off
-
-                @pl.when((k >= 0) & (k < pieces))
+        for p in range(2):
+            far_off = distance[p]
+            k = tau - DEPTH * far_off
+
+            @pl.when((k >= 0) & (k < pieces))
+            def _():
+                @pl.when(far_off > 0)
                 def _():
-                    @pl.when(far_off > 0)
-                    def _():
-                        hop(s, p, k).wait_recv()
-
-                    @pl.when(far_off < n_real - 1)
-                    def _():
-                        hop(s, p, k).start()
-
-                    edge_hop(s, p, k).start()
-
-        done = tau - (n_real - 1) - LAG
+                    hop(p, k).wait_recv()
+
+                @pl.when(far_off < n_real - 1)
+                def _():
+                    hop(p, k).start()
+
+                edge_hop(1, p, k).start()
+
+        for p in range(2):
+            @pl.when(tau < DEPTH)
+            def _():
+                sent[p, rows_of(tau), :] = own[p, rows_of(tau), :]
+
+            @pl.when((tau >= DEPTH) & (tau < slots_sent + DEPTH))
+            def _():
+                pass_on(p, tau - DEPTH).wait_recv()
+
+            @pl.when((tau >= DEPTH) & (tau < slots_sent))
+            def _():
+                mine = own[p, rows_of(jnp.minimum(tau, pieces - 1)), :]
+                sent[p, rows_of(tau), :] = jnp.where(from_owner[p] == 0, mine, got[p, rows_of(tau - DEPTH), :])
+
+            @pl.when(tau < slots_sent)
+            def _():
+                pass_on(p, tau).start()
+
+            @pl.when((tau >= (n_real - 1) * DEPTH) & (tau < slots_sent + DEPTH))
+            def _():
+                k = tau - (n_real - 1) * DEPTH
+                piece = own[p, rows_of(k), :]
+                for d in range(1, n_real):
+                    piece = jnp.where(from_owner[p] == d, got[p, rows_of(k + (d - 1) * DEPTH), :], piece)
+                field[0, p, rows_of(k), :] = piece
+                edge_hop(0, p, k).start()
+
+        done = tau - (n_real - 1) * DEPTH - LAG
 
         @pl.when(done == 0)
         def _():
@@ -263,7 +297,7 @@
 
         return carry
 
-    lax.fori_loop(0, pieces + n_real - 1 + LAG, step, 0)
+    lax.fori_loop(0, pieces + (n_real - 1) * DEPTH + LAG, step, 0)
 
     for s in range(2):
         for p in range(2):
@@ -310,6 +344,29 @@
     for i in range(1, n_far):
         far_hop(i).wait_recv()
 
+    for p in range(2):
+        root_hop(p).wait_send()
+    for i in range(1, n_near):
+        near_hop(i).wait_send()
+    for i in range(1, n_far):
+        far_hop(i).wait_send()
+
+    def whole(s, p, sem):
+        return pltpu.make_async_copy(field.at[s, p], field.at[s, p], sem)
+
+    for p in range(2):
+        for s in range(2):
+            whole(s, p, edge_send.at[s, p]).wait()
+
+        @pl.when(distance[p] < n_real - 1)
+        def _():
+            whole(1, p, send_sem.at[p]).wait()
+
+        pltpu.make_async_copy(sent.at[p], sent.at[p], sent_sem.at[p]).wait()
+
+
+def finish_kernel(image, load, far, order, red, res, nrm, out, sems, *, cells):
+    planes, circ, axial = load.shape
     group = lax.broadcasted_iota(jnp.int32, (1, LANES), 1) // 32
     rows = [far[:, r, :] for r in range(8)]
 
@@ -323,7 +380,7 @@
     def shared(x):
         return one(jnp.sum(x, axis=0, keepdims=True), 2) / cells
 
-    swapped = picks[0] == last
+    swapped = order[0:1, :] > 0.5
     r00, r01, r11 = jnp.where(swapped, rows[2], rows[0]), rows[1], jnp.where(swapped, rows[0], rows[2])
     f0, f1 = jnp.where(swapped, rows[4], rows[3]), jnp.where(swapped, rows[3], rows[4])
     norm0 = shared(r00)
@@ -348,6 +405,32 @@
     )
     spot = lax.broadcasted_iota(jnp.int32, (1, LANES), 1)
 
+    scale = [[jnp.sum(jnp.where(spot == 32 * t, g, 0.0), axis=1, keepdims=True) for g in (g0, g1)] for t in range(2)]
+    blocks = 8
+    tall = circ // blocks
+
+    def out_copy(t, b):
+        rows = pl.ds(pl.multiple_of(b * tall, tall), tall)
+        return pltpu.make_async_copy(out.at[t, :, rows], res.at[t, :, rows], sems.at[t])
+
+    def finish(b, carry):
+        def block(i, c):
+            rows = pl.ds(pl.multiple_of(b * tall + i * 8, 8), 8)
+            for p in range(planes):
+                force = load[p, rows, :]
+                for t in range(2):
+                    out[t, p, rows, :] = force - (
+                        scale[t][0] * image[t, 0, p, rows, :] + scale[t][1] * image[t, 1, p, rows, :]
+                    )
+            return c
+
+        lax.fori_loop(0, tall // 8, block, 0)
+        for t in range(2):
+            out_copy(t, b).start()
+        return carry
+
+    lax.fori_loop(0, blocks, finish, 0)
+
     def scalar(x, t):
         return jnp.sum(jnp.where(spot == 32 * t, x, 0.0))
 
@@ -358,52 +441,8 @@
         red[t, 1, 1] = scalar(a11, t)
         nrm[t] = scalar(square, t)
 
-    scale = [[jnp.sum(jnp.where(spot == 32 * t, g, 0.0), axis=1, keepdims=True) for g in (g0, g1)] for t in range(2)]
-    blocks = 8
-    tall = circ // blocks
-
-    def out_copy(t, b):
-        rows = pl.ds(pl.multiple_of(b * tall, tall), tall)
-        return pltpu.make_async_copy(image.at[t, 0, :, rows], res.at[t, :, rows], local_sem.at[4 + t])
-
-    def finish(b, carry):
-        def block(i, c):
-            rows = pl.ds(pl.multiple_of(b * tall + i * 8, 8), 8)
-            for p in range(planes):
-                force = load[p, rows, :]
-                for t in range(2):
-                    image[t, 0, p, rows, :] = force - (
-                        scale[t][0] * image[t, 0, p, rows, :] + scale[t][1] * image[t, 1, p, rows, :]
-                    )
-            return c
-
-        lax.fori_loop(0, tall // 8, block, 0)
-        for t in range(2):
-            out_copy(t, b).start()
-        return carry
-
-    lax.fori_loop(0, blocks, finish, 0)
-
-    for p in range(2):
-        root_hop(p).wait_send()
-    for i in range(1, n_near):
-        near_hop(i).wait_send()
-    for i in range(1, n_far):
-        far_hop(i).wait_send()
-
-    def whole(s, p, sem):
-        return pltpu.make_async_copy(field.at[s, p], field.at[s, p], sem)
-
-    for s in range(2):
-        for p in range(2):
-            whole(s, p, edge_send.at[s, p]).wait()
-
-            @pl.when(distance[s][p] < n_real - 1)
-            def _():
-                whole(s, p, send_sem.at[s, p]).wait()
-
     for t in range(2):
-        pltpu.make_async_copy(image.at[t, 0], res.at[t], local_sem.at[4 + t]).wait()
+        pltpu.make_async_copy(out.at[t], res.at[t], sems.at[t]).wait()
 
 
 def shards(snapshots, load, base_modulus, mistune, material_ids, realization_map, picks):
@@ -415,55 +454,71 @@
     vmem = lambda *shape: pltpu.VMEM(shape, F32)
     dma = lambda *shape: pltpu.SemaphoreType.DMA(shape)
 
-    def run(owner):
-        return pl.pallas_call(
-            functools.partial(kernel, owner),
-            out_shape=(
-                jax.ShapeDtypeStruct((2, 2, 2), F32),
-                jax.ShapeDtypeStruct((2, planes, circ, axial), F32),
-                jax.ShapeDtypeStruct((2,), F32),
-            ),
-            in_specs=[pl.BlockSpec(memory_space=pltpu.SMEM)] * 4 + [pl.BlockSpec(memory_space=pl.ANY)] * 3,
-            out_specs=(
-                pl.BlockSpec(memory_space=pltpu.SMEM),
-                pl.BlockSpec(memory_space=pl.ANY),
-                pl.BlockSpec(memory_space=pltpu.SMEM),
-            ),
-            scratch_shapes=[
-                vmem(2, planes, circ, axial),
-                vmem(2, 2, circ, axial),
-                vmem(held, planes, circ, axial),
-                vmem(planes, circ, axial),
-                vmem(planes, circ, axial),
-                vmem(2, circ, axial),
-                vmem(2, planes, circ + 2 * PAD, axial),
-                vmem(2, 2, planes, circ, axial),
-                vmem(2, circ + 2 * PAD, LANES),
-                vmem(2, 2, circ, LANES),
-                vmem(24, 8, LANES),
-                vmem(n_near, 8, LANES),
-                vmem(n_far, 8, LANES),
-                dma(6),
-                dma(2, 2),
-                dma(2, 2, pieces),
-                dma(2, 2),
-                dma(2, 2, pieces),
-                dma(2),
-                dma(2),
-                dma(n_near),
-                dma(n_near),
-                dma(n_far),
-                dma(n_far),
-            ],
-            compiler_params=pltpu.CompilerParams(
-                collective_id=owner, has_side_effects=True, vmem_limit_bytes=40 * 2**20
-            ),
-        )(picks, mistune, material_ids, realization_map, snapshots, load, base_modulus)
-
-    other = jnp.minimum(picks[0], picks[1])
-    return lax.switch(
-        lax.div(other, jnp.int32(held)), [lambda owner=owner: run(owner) for owner in range(n_real)]
-    )
+    kept = pieces + (n_real - 2) * DEPTH
+    whole = lambda space, count: [pl.BlockSpec(memory_space=space)] * count
+    sums = pl.pallas_call(
+        gather_kernel,
+        out_shape=(
+            vmem(2, 2, planes, circ, axial),
+            vmem(planes, circ, axial),
+            vmem(n_far, 8, LANES),
+            vmem(8, LANES),
+        ),
+        in_specs=whole(pltpu.HBM, 7),
+        out_specs=tuple(whole(pltpu.VMEM, 4)),
+        scratch_shapes=[
+            pltpu.SMEM(picks.shape, jnp.int32),
+            pltpu.SMEM(mistune.shape, F32),
+            pltpu.SMEM(material_ids.shape, jnp.int32),
+            pltpu.SMEM(realization_map.shape, jnp.int32),
+            vmem(2, planes, circ, axial),
+            vmem(2, 2, circ, axial),
+            vmem(held, planes, circ, axial),
+            vmem(planes, circ, axial),
+            vmem(planes, kept * ROWS, axial),
+            vmem(planes, kept * ROWS, axial),
+            vmem(planes, circ, axial),
+            vmem(2, circ, axial),
+            vmem(2, planes, circ + 2 * PAD, axial),
+            vmem(2, circ + 2 * PAD, LANES),
+            vmem(2, 2, circ, LANES),
+            vmem(24, 8, LANES),
+            vmem(n_near, 8, LANES),
+            dma(4),
+            dma(4),
+            dma(2),
+            dma(2, pieces),
+            dma(2),
+            dma(2, kept),
+            dma(2, 2),
+            dma(2, 2, pieces),
+            dma(2),
+            dma(2),
+            dma(n_near),
+            dma(n_near),
+            dma(n_far),
+            dma(n_far),
+        ],
+        compiler_params=pltpu.CompilerParams(
+            collective_id=0, has_side_effects=True, vmem_limit_bytes=58720256
+        ),
+    )(picks, mistune, material_ids, realization_map, snapshots, load, base_modulus)
+    return pl.pallas_call(
+        functools.partial(finish_kernel, cells=float(planes * n_span * circ * axial)),
+        out_shape=(
+            jax.ShapeDtypeStruct((2, 2, 2), F32),
+            jax.ShapeDtypeStruct((2, planes, circ, axial), F32),
+            jax.ShapeDtypeStruct((2,), F32),
+        ),
+        in_specs=whole(pltpu.VMEM, 4),
+        out_specs=(
+            pl.BlockSpec(memory_space=pltpu.SMEM),
+            pl.BlockSpec(memory_space=pltpu.HBM),
+            pl.BlockSpec(memory_space=pltpu.SMEM),
+        ),
+        scratch_shapes=[vmem(2, planes, circ, axial), dma(2)],
+        compiler_params=pltpu.CompilerParams(vmem_limit_bytes=40 * 2**20),
+    )(*sums)
 
 
 def solution(mesh):

time: 83.5 us -> 59.2 us (0.71)
  Pallas kernels: 77.6 us -> 58.4 us
  local copies, waits for them, and re-layouts: 3.72 us -> 0 us
  between operations: 1.95 us -> 0.64 us
    pallas_call x1 -> x2, Pallas kernels: 77.6 us -> 58.4 us  [the longest x1 56 us: shards(): pl.pallas_call(gather_kernel, out_shape=(vmem(2, 2, planes, circ, axial),...]
    unnamed x3 -> x0, local copies, waits for them, and re-layouts: 2.41 us -> none
    slice x1 -> x0, local copies, waits for them, and re-layouts: 1.31 us -> none  [shards(): other = jnp.minimum(picks[0], picks[1])]
where the time goes in v2:
time: 59.2 us; the launch traced here: 59.1 us
  Pallas kernels  58.4 us (99%)
  between operations  0.64 us (1%)
    pallas_call x1, Pallas kernels, shards(): pl.pallas_call(gather_kernel, out_shape=(vmem(2, 2, planes, circ, axial),...  56 us
    pallas_call x1, Pallas kernels, shards(): pl.pallas_call(functools.partial(finish_kernel, cells=float(planes * n_sp...  2.41 us

profile of v2, /device:TPU:1, one launch (start us, length us, event | category | flops | bytes accessed | tf_op | source)
XLA Modules:
  0.0 59.1 jit_solution(11249284865583574980)
XLA Ops:
  0.6 56.0 %shard_map.94 = (f32[2,2,2,512,256]{4,3,2,1,0:T(8,128)S(1)}, f32[2,512,256]{2,1,0:T(8,128)S(1)}, f32[4,8,128]{2,1,0:T(8,128)S(1)}, f32[8,128]{1,0:T(8,128)S(1)}) custom-call(s32[2]{0:T(128)} %picks_in.1, f32[8]{0:T(128)} %mistune_in.1, s32[8,32]{1,0:T(8,128)} %ids_in.1, s32[2]{0:T(128)} %slots_in.1, f32[2,2,512,256]{3,2,1,0:T(8,128)} %snaps.1, ...), custom_call_target="tpu_custom_call" | custom-call | tf_op jit(solution)/shard_map/pallas_call | solution.py:459
  56.6 2.4 %shard_map.95 = (f32[2,2,2]{2,1,0:T(2,128)}, f32[2,2,512,256]{3,2,1,0:T(8,128)}, f32[2]{0:T(128)}) custom-call(f32[2,2,2,512,256]{4,3,2,1,0:T(8,128)S(1)} %get-tuple-element.7.image, f32[2,512,256]{2,1,0:T(8,128)S(1)} %get-tuple-element.8.load, f32[4,8,128]{2,1,0:T(8,128)S(1)} %get-tuple-element.9.far, f32[8,128]{1,0:T(8,128)S(1)} %get-tuple-element.10.order), custom_call_target="tpu_custom_call" | custom-call | tf_op jit(solution)/shard_map/pallas_call | solution.py:506

commit v3 on v2

--- a/solution.py
+++ b/solution.py
@@ -10,8 +10,8 @@
 MESH = pl.DeviceIdType.MESH
 SHIFT = 0.5
 ROWS = 32
-DEPTH = 2
-LAG = 2
+DEPTH = 3
+LAG = 1
 PAD = 8
 LANES = 128
 F32 = jnp.float32
@@ -21,9 +21,9 @@
     picks_in, mistune_in, ids_in, slots_in, snaps, load_in, base_in,
     image, load, far, order,
     picks, mistune, ids, slots,
-    field, edge, both, own, sent, got, root, root_edge, mixed, factor, pair, totals, near,
+    field, edge, both, own, sent, got, root, root_edge, mixed, factor, pair, totals, mate, hub,
     small_sem, local_sem, send_sem, recv_sem, sent_sem, got_sem, edge_send, edge_recv, root_send, root_recv,
-    near_send, near_recv, far_send, far_recv,
+    mate_send, mate_recv, hub_send, hub_recv,
 ):
     n_span, n_real = lax.axis_size("span"), lax.axis_size("real")
     span, real = lax.axis_index("span"), lax.axis_index("real")
@@ -33,29 +33,24 @@
     pieces = circ // ROWS
     last = held * n_real - 1
     slots_sent = pieces + (n_real - 2) * DEPTH
-    n_near, n_far = near.shape[0], far.shape[0]
-
     before, after = lax.rem(span + n_span - 1, n_span), lax.rem(span + 1, n_span)
     below, above = lax.rem(real + n_real - 1, n_real), lax.rem(real + 1, n_real)
-    my_far, my_near = lax.div(span, n_near), lax.rem(span, n_near)
-
-    def near_peer(i):
-        return my_far * n_near + lax.rem(my_near + i, n_near)
-
-    def far_peer(i):
-        return lax.rem(my_far + i, n_far) * n_near + my_near
+    core, chip, chips = lax.rem(span, 2), lax.div(span, 2), n_span // 2
+    outer, inner = core, 1 - core
+    hubs = chips // 2
+
+    def partner(step):
+        return 2 * lax.rem(chip + core * hubs + step, chips) + core
 
     barrier = pltpu.get_barrier_semaphore()
-    greeted = 0
     for where in [{"real": below}, {"real": above}, {"span": before}, {"span": after}]:
         pl.semaphore_signal(barrier, inc=1, device_id=where, device_id_type=MESH)
-        greeted += 1
-    for i in range(1, n_near):
-        pl.semaphore_signal(barrier, inc=1, device_id={"span": near_peer(i)}, device_id_type=MESH)
-        greeted += 1
-    for i in range(1, n_far):
-        pl.semaphore_signal(barrier, inc=1, device_id={"span": far_peer(i)}, device_id_type=MESH)
-        greeted += 1
+    for i in range(hubs):
+        source = 2 * lax.rem(chip + chips - (core * hubs + i), chips) + core
+
+        @pl.when(core * hubs + i > 0)
+        def _():
+            pl.semaphore_signal(barrier, inc=1, device_id={"span": source}, device_id_type=MESH)
 
     smalls = [
         pltpu.make_async_copy(src, dst, small_sem.at[i])
@@ -80,21 +75,6 @@
     other = jnp.minimum(picks[0], picks[1])
     order[...] = jnp.full(order.shape, jnp.where(picks[0] == last, 1.0, 0.0), F32)
 
-    def fill(j, carry):
-        for t in range(2):
-            value = mistune[ids[slots[t], j]]
-            factor[t, pl.ds(PAD + j * width, width), :] = jnp.full((width, LANES), value, F32)
-        return carry
-
-    lax.fori_loop(0, sectors, fill, 0)
-    for t in range(2):
-        factor[t, 0:PAD, :] = factor[t, circ : circ + PAD, :]
-        factor[t, circ + PAD : circ + 2 * PAD, :] = factor[t, PAD : 2 * PAD, :]
-        here = factor[t, PAD : circ + PAD, :]
-        for side, shift in ((0, -1), (1, 1)):
-            pair[t, side] = jnp.sqrt(here * factor[t, PAD + shift : circ + PAD + shift, :])
-    totals[...] = jnp.zeros_like(totals)
-
     base_copy.wait()
     both_copy.wait()
     chosen = lax.rem(other, held)
@@ -112,7 +92,7 @@
     def _():
         last_copy.wait()
 
-    pl.semaphore_wait(barrier, greeted)
+    pl.semaphore_wait(barrier, 4 + hubs - 1 + core)
 
     def root_hop(p):
         return pltpu.make_async_remote_copy(
@@ -130,13 +110,37 @@
     def rows_of(k):
         return pl.ds(pl.multiple_of(k * ROWS, ROWS), ROWS)
 
+    half = pieces // 2
+
+    def plane_of(k):
+        return jnp.where(k < half, outer, inner)
+
+    def place(p, k):
+        return rows_of(p * half + lax.rem(k, half))
+
+    def prepare():
+        def fill(j, carry):
+            for t in range(2):
+                value = mistune[ids[slots[t], j]]
+                factor[t, pl.ds(PAD + j * width, width), :] = jnp.full((width, LANES), value, F32)
+            return carry
+
+        lax.fori_loop(0, sectors, fill, 0)
+        for t in range(2):
+            factor[t, 0:PAD, :] = factor[t, circ : circ + PAD, :]
+            factor[t, circ + PAD : circ + 2 * PAD, :] = factor[t, PAD : 2 * PAD, :]
+            here = factor[t, PAD : circ + PAD, :]
+            for side, shift in ((0, -1), (1, 1)):
+                pair[t, side] = jnp.sqrt(here * factor[t, PAD + shift : circ + PAD + shift, :])
+        totals[...] = jnp.zeros_like(totals)
+
     def along(p):
         return {"real": above if p == 0 else below}
 
     def hop(p, k):
         return pltpu.make_async_remote_copy(
-            src_ref=field.at[1, p, rows_of(k)],
-            dst_ref=field.at[1, p, rows_of(k)],
+            src_ref=field.at[1, plane_of(k), place(p, k)],
+            dst_ref=field.at[1, plane_of(k), place(p, k)],
             send_sem=send_sem.at[p],
             recv_sem=recv_sem.at[p, k],
             device_id=along(p),
@@ -154,14 +158,19 @@
         )
 
     def edge_hop(s, p, k):
+        plane = plane_of(k)
         return pltpu.make_async_remote_copy(
-            src_ref=field.at[s, p, rows_of(k)],
-            dst_ref=edge.at[s, 1 - p, rows_of(k)],
+            src_ref=field.at[s, plane, place(p, k)],
+            dst_ref=edge.at[s, 1 - plane, place(p, k)],
             send_sem=edge_send.at[s, p],
-            recv_sem=edge_recv.at[s, 1 - p, k],
-            device_id={"span": before if p == 0 else after},
+            recv_sem=edge_recv.at[s, p, k],
+            device_id={"span": jnp.where(plane == 0, before, after)},
             device_id_type=MESH,
         )
+
+    def edge_arrives(s, p, k):
+        here = edge.at[s, plane_of(k), place(p, k)]
+        pltpu.make_async_copy(here, here, edge_recv.at[s, p, k]).wait()
 
     distance = (real + 1) % n_real, n_real - 1 - real
     owner = lax.div(other, held)
@@ -173,7 +182,11 @@
     not_first, not_last = column > 0, column < axial - 1
 
     def mix(k, carry):
-        start = pl.multiple_of(k * 8, 8)
+        for p in range(2):
+            mix_rows(pl.multiple_of(p * (circ // 2) + k * 8, 8))
+        return carry
+
+    def mix_rows(start):
         rows = pl.ds(start, 8)
         q0, q1, ql, qh = root[0, rows, :], root[1, rows, :], root_edge[0, rows, :], root_edge[1, rows, :]
         for s in range(2):
@@ -183,7 +196,6 @@
                 left = jnp.where(not_first, pltpu.roll(across, 1, 1), 0.0)
                 right = jnp.where(not_last, pltpu.roll(across, axial - 1, 1), 0.0)
                 mixed[s, p, pl.ds(start + PAD, 8), :] = across + 0.5 * (left + right)
-        return carry
 
     def fold(x):
         return x[:, :LANES] + x[:, LANES:]
@@ -254,7 +266,7 @@
         for p in range(2):
             @pl.when(tau < DEPTH)
             def _():
-                sent[p, rows_of(tau), :] = own[p, rows_of(tau), :]
+                sent[p, rows_of(tau), :] = own[plane_of(tau), place(p, tau), :]
 
             @pl.when((tau >= DEPTH) & (tau < slots_sent + DEPTH))
             def _():
@@ -262,7 +274,8 @@
 
             @pl.when((tau >= DEPTH) & (tau < slots_sent))
             def _():
-                mine = own[p, rows_of(jnp.minimum(tau, pieces - 1)), :]
+                k = jnp.minimum(tau, pieces - 1)
+                mine = own[plane_of(k), place(p, k), :]
                 sent[p, rows_of(tau), :] = jnp.where(from_owner[p] == 0, mine, got[p, rows_of(tau - DEPTH), :])
 
             @pl.when(tau < slots_sent)
@@ -272,13 +285,17 @@
             @pl.when((tau >= (n_real - 1) * DEPTH) & (tau < slots_sent + DEPTH))
             def _():
                 k = tau - (n_real - 1) * DEPTH
-                piece = own[p, rows_of(k), :]
+                piece = own[plane_of(k), place(p, k), :]
                 for d in range(1, n_real):
                     piece = jnp.where(from_owner[p] == d, got[p, rows_of(k + (d - 1) * DEPTH), :], piece)
-                field[0, p, rows_of(k), :] = piece
+                field[0, plane_of(k), place(p, k), :] = piece
                 edge_hop(0, p, k).start()
 
-        done = tau - (n_real - 1) * DEPTH - LAG
+        @pl.when(tau == 0)
+        def _():
+            prepare()
+
+        done = tau - half - (n_real - 1) * DEPTH - LAG
 
         @pl.when(done == 0)
         def _():
@@ -290,10 +307,13 @@
         def _():
             for s in range(2):
                 for p in range(2):
-                    edge_hop(s, p, done).wait_recv()
+                    edge_arrives(s, p, done)
+                    edge_arrives(s, p, half + done)
             lax.fori_loop(done * (ROWS // 8), (done + 1) * (ROWS // 8), mix, 0)
             per = ROWS // width
-            lax.fori_loop(jnp.maximum(done * per - 1, 1), (done + 1) * per - 1, work, 0)
+            first, end = jnp.maximum(done * per - 1, 1), (done + 1) * per - 1
+            for p in range(2):
+                lax.fori_loop(p * (sectors // 2) + first, p * (sectors // 2) + end, work, 0)
 
         return carry
 
@@ -303,7 +323,8 @@
         for p in range(2):
             mixed[s, p, 0:PAD, :] = mixed[s, p, circ : circ + PAD, :]
             mixed[s, p, circ + PAD : circ + 2 * PAD, :] = mixed[s, p, PAD : 2 * PAD, :]
-    lax.fori_loop(0, 2, lambda i, c: work((1 - i) * (sectors - 1), c), 0)
+    ends = sectors // 2 - 1
+    lax.fori_loop(0, 4, lambda i, c: work(lax.div(i, 2) * (ends + 1) + lax.rem(i, 2) * ends, c), 0)
 
     lane = lax.broadcasted_iota(jnp.int32, (8, LANES), 1)
     packed = jnp.zeros((8, LANES), F32)
@@ -313,43 +334,58 @@
         v = v + pltpu.roll(v, 32, 1)
         packed = jnp.where((lane >= 32 * g) & (lane < 32 * g + 32), v, packed)
 
-    def near_hop(i):
+    def mate_hop(i, src, dst):
         return pltpu.make_async_remote_copy(
-            src_ref=near.at[my_near],
-            dst_ref=near.at[my_near],
-            send_sem=near_send.at[i],
-            recv_sem=near_recv.at[i],
-            device_id={"span": near_peer(i)},
+            src_ref=src,
+            dst_ref=dst,
+            send_sem=mate_send.at[i],
+            recv_sem=mate_recv.at[i],
+            device_id={"span": span + 1 - 2 * core},
             device_id_type=MESH,
         )
 
-    def far_hop(i):
+    def hub_hop(i):
         return pltpu.make_async_remote_copy(
-            src_ref=far.at[my_far],
-            dst_ref=far.at[my_far],
-            send_sem=far_send.at[i],
-            recv_sem=far_recv.at[i],
-            device_id={"span": far_peer(i)},
+            src_ref=mate.at[2],
+            dst_ref=hub.at[i],
+            send_sem=hub_send.at[i],
+            recv_sem=hub_recv.at[i],
+            device_id={"span": partner(i)},
             device_id_type=MESH,
         )
 
-    near[my_near] = packed
-    for i in range(1, n_near):
-        near_hop(i).start()
-    for i in range(1, n_near):
-        near_hop(i).wait_recv()
-    far[my_far] = jnp.sum(near[...], axis=0)
-    for i in range(1, n_far):
-        far_hop(i).start()
-    for i in range(1, n_far):
-        far_hop(i).wait_recv()
+    mate[0] = packed
+    first_meeting = mate_hop(0, mate.at[0], mate.at[1])
+    first_meeting.start()
+    first_meeting.wait_recv()
+    mate[2] = mate[0] + mate[1]
+    for i in range(hubs):
+        @pl.when(core * hubs + i > 0)
+        def _():
+            hub_hop(i).start()
+
+    @pl.when(core == 0)
+    def _():
+        hub[0] = mate[2]
+
+    for i in range(hubs):
+        @pl.when(core * hubs + i > 0)
+        def _():
+            hub_hop(i).wait_recv()
+
+    far[core] = jnp.sum(hub[...], axis=0)
+    last_meeting = mate_hop(1, far.at[core], far.at[core])
+    last_meeting.start()
+    last_meeting.wait_recv()
 
     for p in range(2):
         root_hop(p).wait_send()
-    for i in range(1, n_near):
-        near_hop(i).wait_send()
-    for i in range(1, n_far):
-        far_hop(i).wait_send()
+    first_meeting.wait_send()
+    last_meeting.wait_send()
+    for i in range(hubs):
+        @pl.when(core * hubs + i > 0)
+        def _():
+            hub_hop(i).wait_send()
 
     def whole(s, p, sem):
         return pltpu.make_async_copy(field.at[s, p], field.at[s, p], sem)
@@ -448,8 +484,7 @@
 def shards(snapshots, load, base_modulus, mistune, material_ids, realization_map, picks):
     n_span, n_real = lax.axis_size("span"), lax.axis_size("real")
     held, planes, circ, axial = snapshots.shape
-    n_near = 8 if n_span % 8 == 0 else 2
-    n_far = n_span // n_near
+    hubs = n_span // 4
     pieces = circ // ROWS
     vmem = lambda *shape: pltpu.VMEM(shape, F32)
     dma = lambda *shape: pltpu.SemaphoreType.DMA(shape)
@@ -461,7 +496,7 @@
         out_shape=(
             vmem(2, 2, planes, circ, axial),
             vmem(planes, circ, axial),
-            vmem(n_far, 8, LANES),
+            vmem(2, 8, LANES),
             vmem(8, LANES),
         ),
         in_specs=whole(pltpu.HBM, 7),
@@ -483,7 +518,8 @@
             vmem(2, circ + 2 * PAD, LANES),
             vmem(2, 2, circ, LANES),
             vmem(24, 8, LANES),
-            vmem(n_near, 8, LANES),
+            vmem(3, 8, LANES),
+            vmem(hubs, 8, LANES),
             dma(4),
             dma(4),
             dma(2),
@@ -494,10 +530,10 @@
             dma(2, 2, pieces),
             dma(2),
             dma(2),
-            dma(n_near),
-            dma(n_near),
-            dma(n_far),
-            dma(n_far),
+            dma(2),
+            dma(2),
+            dma(hubs),
+            dma(hubs),
         ],
         compiler_params=pltpu.CompilerParams(
             collective_id=0, has_side_effects=True, vmem_limit_bytes=58720256

time: 59.2 us -> 54.8 us (0.926)
  Pallas kernels: 58.4 us -> 54.1 us
    pallas_call x1, Pallas kernels: 56 us -> 51.7 us  [shards(): pl.pallas_call(gather_kernel, out_shape=(vmem(2, 2, planes, circ, axial),...]
where the time goes in v3:
time: 54.8 us; the launch traced here: 54.7 us
  Pallas kernels  54.1 us (99%)
  between operations  0.64 us (1%)
    pallas_call x1, Pallas kernels, shards(): pl.pallas_call(gather_kernel, out_shape=(vmem(2, 2, planes, circ, axial),...  51.7 us
    pallas_call x1, Pallas kernels, shards(): pl.pallas_call(functools.partial(finish_kernel, cells=float(planes * n_sp...  2.41 us

profile of v3, /device:TPU:1, one launch (start us, length us, event | category | flops | bytes accessed | tf_op | source)
XLA Modules:
  0.0 54.7 jit_solution(18075328515196947176)
XLA Ops:
  0.6 51.7 %shard_map.94 = (f32[2,2,2,512,256]{4,3,2,1,0:T(8,128)S(1)}, f32[2,512,256]{2,1,0:T(8,128)S(1)}, f32[2,8,128]{2,1,0:T(8,128)S(1)}, f32[8,128]{1,0:T(8,128)S(1)}) custom-call(s32[2]{0:T(128)} %picks_in.1, f32[8]{0:T(128)} %mistune_in.1, s32[8,32]{1,0:T(8,128)} %ids_in.1, s32[2]{0:T(128)} %slots_in.1, f32[2,2,512,256]{3,2,1,0:T(8,128)} %snaps.1, ...), custom_call_target="tpu_custom_call" | custom-call | tf_op jit(solution)/shard_map/pallas_call | solution.py:494
  52.3 2.4 %shard_map.95 = (f32[2,2,2]{2,1,0:T(2,128)}, f32[2,2,512,256]{3,2,1,0:T(8,128)}, f32[2]{0:T(128)}) custom-call(f32[2,2,2,512,256]{4,3,2,1,0:T(8,128)S(1)} %get-tuple-element.7.image, f32[2,512,256]{2,1,0:T(8,128)S(1)} %get-tuple-element.8.load, f32[2,8,128]{2,1,0:T(8,128)S(1)} %get-tuple-element.9.far, f32[8,128]{1,0:T(8,128)S(1)} %get-tuple-element.10.order), custom_call_target="tpu_custom_call" | custom-call | tf_op jit(solution)/shard_map/pallas_call | solution.py:542

commit v4 on v3

--- a/solution.py
+++ b/solution.py
@@ -37,20 +37,18 @@
     below, above = lax.rem(real + n_real - 1, n_real), lax.rem(real + 1, n_real)
     core, chip, chips = lax.rem(span, 2), lax.div(span, 2), n_span // 2
     outer, inner = core, 1 - core
-    hubs = chips // 2
+    hubs = chips
 
     def partner(step):
-        return 2 * lax.rem(chip + core * hubs + step, chips) + core
+        return 2 * lax.rem(chip + step, chips) + core
 
     barrier = pltpu.get_barrier_semaphore()
     for where in [{"real": below}, {"real": above}, {"span": before}, {"span": after}]:
         pl.semaphore_signal(barrier, inc=1, device_id=where, device_id_type=MESH)
-    for i in range(hubs):
-        source = 2 * lax.rem(chip + chips - (core * hubs + i), chips) + core
-
-        @pl.when(core * hubs + i > 0)
-        def _():
-            pl.semaphore_signal(barrier, inc=1, device_id={"span": source}, device_id_type=MESH)
+    for i in range(1, hubs):
+        source = 2 * lax.rem(chip + chips - i, chips) + core
+
+        pl.semaphore_signal(barrier, inc=1, device_id={"span": source}, device_id_type=MESH)
 
     smalls = [
         pltpu.make_async_copy(src, dst, small_sem.at[i])
@@ -75,24 +73,22 @@
     other = jnp.minimum(picks[0], picks[1])
     order[...] = jnp.full(order.shape, jnp.where(picks[0] == last, 1.0, 0.0), F32)
 
-    base_copy.wait()
     both_copy.wait()
     chosen = lax.rem(other, held)
 
-    def take_root(i, carry):
+    def choose_own(i, carry):
         rows = pl.ds(pl.multiple_of(i * 16, 16), 16)
         for p in range(planes):
-            root[p, rows, :] = jnp.sqrt(root[p, rows, :])
             own[p, rows, :] = jnp.where(chosen == 0, both[0, p, rows, :], both[held - 1, p, rows, :])
         return carry
 
-    lax.fori_loop(0, circ // 16, take_root, 0)
+    lax.fori_loop(0, circ // 16, choose_own, 0)
 
     @pl.when(real == n_real - 1)
     def _():
         last_copy.wait()
 
-    pl.semaphore_wait(barrier, 4 + hubs - 1 + core)
+    pl.semaphore_wait(barrier, 4 + hubs - 1)
 
     def root_hop(p):
         return pltpu.make_async_remote_copy(
@@ -104,9 +100,6 @@
             device_id_type=MESH,
         )
 
-    for p in range(2):
-        root_hop(p).start()
-
     def rows_of(k):
         return pl.ds(pl.multiple_of(k * ROWS, ROWS), ROWS)
 
@@ -119,6 +112,18 @@
         return rows_of(p * half + lax.rem(k, half))
 
     def prepare():
+        base_copy.wait()
+
+        def take_root(i, carry):
+            rows = pl.ds(pl.multiple_of(i * 16, 16), 16)
+            for p in range(planes):
+                root[p, rows, :] = jnp.sqrt(root[p, rows, :])
+            return carry
+
+        lax.fori_loop(0, circ // 16, take_root, 0)
+        for p in range(2):
+            root_hop(p).start()
+
         def fill(j, carry):
             for t in range(2):
                 value = mistune[ids[slots[t], j]]
@@ -248,22 +253,6 @@
 
     def step(tau, carry):
         for p in range(2):
-            far_off = distance[p]
-            k = tau - DEPTH * far_off
-
-            @pl.when((k >= 0) & (k < pieces))
-            def _():
-                @pl.when(far_off > 0)
-                def _():
-                    hop(p, k).wait_recv()
-
-                @pl.when(far_off < n_real - 1)
-                def _():
-                    hop(p, k).start()
-
-                edge_hop(1, p, k).start()
-
-        for p in range(2):
             @pl.when(tau < DEPTH)
             def _():
                 sent[p, rows_of(tau), :] = own[plane_of(tau), place(p, tau), :]
@@ -290,6 +279,22 @@
                     piece = jnp.where(from_owner[p] == d, got[p, rows_of(k + (d - 1) * DEPTH), :], piece)
                 field[0, plane_of(k), place(p, k), :] = piece
                 edge_hop(0, p, k).start()
+
+        for p in range(2):
+            far_off = distance[p]
+            k = tau - DEPTH * far_off
+
+            @pl.when((k >= 0) & (k < pieces))
+            def _():
+                @pl.when(far_off > 0)
+                def _():
+                    hop(p, k).wait_recv()
+
+                @pl.when(far_off < n_real - 1)
+                def _():
+                    hop(p, k).start()
+
+                edge_hop(1, p, k).start()
 
         @pl.when(tau == 0)
         def _():
@@ -359,33 +364,21 @@
     first_meeting.start()
     first_meeting.wait_recv()
     mate[2] = mate[0] + mate[1]
-    for i in range(hubs):
-        @pl.when(core * hubs + i > 0)
-        def _():
-            hub_hop(i).start()
-
-    @pl.when(core == 0)
-    def _():
-        hub[0] = mate[2]
-
-    for i in range(hubs):
-        @pl.when(core * hubs + i > 0)
-        def _():
-            hub_hop(i).wait_recv()
-
-    far[core] = jnp.sum(hub[...], axis=0)
-    last_meeting = mate_hop(1, far.at[core], far.at[core])
-    last_meeting.start()
-    last_meeting.wait_recv()
+    for i in range(1, hubs):
+        hub_hop(i).start()
+
+    hub[0] = mate[2]
+
+    for i in range(1, hubs):
+        hub_hop(i).wait_recv()
+
+    far[0] = jnp.sum(hub[...], axis=0)
 
     for p in range(2):
         root_hop(p).wait_send()
     first_meeting.wait_send()
-    last_meeting.wait_send()
-    for i in range(hubs):
-        @pl.when(core * hubs + i > 0)
-        def _():
-            hub_hop(i).wait_send()
+    for i in range(1, hubs):
+        hub_hop(i).wait_send()
 
     def whole(s, p, sem):
         return pltpu.make_async_copy(field.at[s, p], field.at[s, p], sem)
@@ -484,7 +477,7 @@
 def shards(snapshots, load, base_modulus, mistune, material_ids, realization_map, picks):
     n_span, n_real = lax.axis_size("span"), lax.axis_size("real")
     held, planes, circ, axial = snapshots.shape
-    hubs = n_span // 4
+    hubs = n_span // 2
     pieces = circ // ROWS
     vmem = lambda *shape: pltpu.VMEM(shape, F32)
     dma = lambda *shape: pltpu.SemaphoreType.DMA(shape)
@@ -496,7 +489,7 @@
         out_shape=(
             vmem(2, 2, planes, circ, axial),
             vmem(planes, circ, axial),
-            vmem(2, 8, LANES),
+            vmem(1, 8, LANES),
             vmem(8, LANES),
         ),
         in_specs=whole(pltpu.HBM, 7),
@@ -530,8 +523,8 @@
             dma(2, 2, pieces),
             dma(2),
             dma(2),
-            dma(2),
-            dma(2),
+            dma(1),
+            dma(1),
             dma(hubs),
             dma(hubs),
         ],

time: 54.8 us -> 52.6 us (0.960)
  Pallas kernels: 54.1 us -> 51.9 us
    pallas_call x1, Pallas kernels: 51.7 us -> 49.5 us  [shards(): pl.pallas_call(gather_kernel, out_shape=(vmem(2, 2, planes, circ, axial),...]
where the time goes in v4:
time: 52.6 us; the launch traced here: 52.5 us
  Pallas kernels  51.9 us (99%)
  between operations  0.64 us (1%)
    pallas_call x1, Pallas kernels, shards(): pl.pallas_call(gather_kernel, out_shape=(vmem(2, 2, planes, circ, axial),...  49.5 us
    pallas_call x1, Pallas kernels, shards(): pl.pallas_call(functools.partial(finish_kernel, cells=float(planes * n_sp...  2.39 us

profile of v4, /device:TPU:1, one launch (start us, length us, event | category | flops | bytes accessed | tf_op | source)
XLA Modules:
  0.0 52.5 jit_solution(15526825160691235497)
XLA Ops:
  0.6 49.5 %shard_map.94 = (f32[2,2,2,512,256]{4,3,2,1,0:T(8,128)S(1)}, f32[2,512,256]{2,1,0:T(8,128)S(1)}, f32[1,8,128]{2,1,0:T(8,128)S(1)}, f32[8,128]{1,0:T(8,128)S(1)}) custom-call(s32[2]{0:T(128)} %picks_in.1, f32[8]{0:T(128)} %mistune_in.1, s32[8,32]{1,0:T(8,128)} %ids_in.1, s32[2]{0:T(128)} %slots_in.1, f32[2,2,512,256]{3,2,1,0:T(8,128)} %snaps.1, ...), custom_call_target="tpu_custom_call" | custom-call | tf_op jit(solution)/shard_map/pallas_call | solution.py:487
  50.1 2.4 %shard_map.95 = (f32[2,2,2]{2,1,0:T(2,128)}, f32[2,2,512,256]{3,2,1,0:T(8,128)}, f32[2]{0:T(128)}) custom-call(f32[2,2,2,512,256]{4,3,2,1,0:T(8,128)S(1)} %get-tuple-element.7.image, f32[2,512,256]{2,1,0:T(8,128)S(1)} %get-tuple-element.8.load, f32[1,8,128]{2,1,0:T(8,128)S(1)} %get-tuple-element.9.far, f32[8,128]{1,0:T(8,128)S(1)} %get-tuple-element.10.order), custom_call_target="tpu_custom_call" | custom-call | tf_op jit(solution)/shard_map/pallas_call | solution.py:535

commit v5 on v4

--- a/solution.py
+++ b/solution.py
@@ -82,7 +82,7 @@
             own[p, rows, :] = jnp.where(chosen == 0, both[0, p, rows, :], both[held - 1, p, rows, :])
         return carry
 
-    lax.fori_loop(0, circ // 16, choose_own, 0)
+    lax.fori_loop(0, circ // 16, choose_own, 0, unroll=4)
 
     @pl.when(real == n_real - 1)
     def _():
@@ -120,7 +120,7 @@
                 root[p, rows, :] = jnp.sqrt(root[p, rows, :])
             return carry
 
-        lax.fori_loop(0, circ // 16, take_root, 0)
+        lax.fori_loop(0, circ // 16, take_root, 0, unroll=4)
         for p in range(2):
             root_hop(p).start()
 
@@ -314,7 +314,7 @@
                 for p in range(2):
                     edge_arrives(s, p, done)
                     edge_arrives(s, p, half + done)
-            lax.fori_loop(done * (ROWS // 8), (done + 1) * (ROWS // 8), mix, 0)
+            lax.fori_loop(0, ROWS // 8, lambda i, c: mix(done * (ROWS // 8) + i, c), 0, unroll=True)
             per = ROWS // width
             first, end = jnp.maximum(done * per - 1, 1), (done + 1) * per - 1
             for p in range(2):
@@ -329,7 +329,7 @@
             mixed[s, p, 0:PAD, :] = mixed[s, p, circ : circ + PAD, :]
             mixed[s, p, circ + PAD : circ + 2 * PAD, :] = mixed[s, p, PAD : 2 * PAD, :]
     ends = sectors // 2 - 1
-    lax.fori_loop(0, 4, lambda i, c: work(lax.div(i, 2) * (ends + 1) + lax.rem(i, 2) * ends, c), 0)
+    lax.fori_loop(0, 2, lambda i, c: work(i * (ends + 1) + ends, work(i * (ends + 1), c)), 0)
 
     lane = lax.broadcasted_iota(jnp.int32, (8, LANES), 1)
     packed = jnp.zeros((8, LANES), F32)
@@ -453,7 +453,7 @@
                     )
             return c
 
-        lax.fori_loop(0, tall // 8, block, 0)
+        lax.fori_loop(0, tall // 8, block, 0, unroll=True)
         for t in range(2):
             out_copy(t, b).start()
         return carry

time: 52.6 us -> 51.5 us (0.979)
  Pallas kernels: 51.9 us -> 50.7 us
    pallas_call x1, Pallas kernels: 49.5 us -> 48.5 us  [shards(): pl.pallas_call(gather_kernel, out_shape=(vmem(2, 2, planes, circ, axial),...]
where the time goes in v5:
time: 51.5 us; the launch traced here: 51.4 us
  Pallas kernels  50.7 us (98%)
  between operations  0.64 us (1%)
    pallas_call x1, Pallas kernels, shards(): pl.pallas_call(gather_kernel, out_shape=(vmem(2, 2, planes, circ, axial),...  48.5 us
    pallas_call x1, Pallas kernels, shards(): pl.pallas_call(functools.partial(finish_kernel, cells=float(planes * n_sp...  2.25 us

profile of v5, /device:TPU:1, one launch (start us, length us, event | category | flops | bytes accessed | tf_op | source)
XLA Modules:
  0.0 51.4 jit_solution(3482091202089743911)
XLA Ops:
  0.6 48.5 %shard_map.94 = (f32[2,2,2,512,256]{4,3,2,1,0:T(8,128)S(1)}, f32[2,512,256]{2,1,0:T(8,128)S(1)}, f32[1,8,128]{2,1,0:T(8,128)S(1)}, f32[8,128]{1,0:T(8,128)S(1)}) custom-call(s32[2]{0:T(128)} %picks_in.1, f32[8]{0:T(128)} %mistune_in.1, s32[8,32]{1,0:T(8,128)} %ids_in.1, s32[2]{0:T(128)} %slots_in.1, f32[2,2,512,256]{3,2,1,0:T(8,128)} %snaps.1, ...), custom_call_target="tpu_custom_call" | custom-call | tf_op jit(solution)/shard_map/pallas_call | solution.py:487
  49.1 2.2 %shard_map.95 = (f32[2,2,2]{2,1,0:T(2,128)}, f32[2,2,512,256]{3,2,1,0:T(8,128)}, f32[2]{0:T(128)}) custom-call(f32[2,2,2,512,256]{4,3,2,1,0:T(8,128)S(1)} %get-tuple-element.7.image, f32[2,512,256]{2,1,0:T(8,128)S(1)} %get-tuple-element.8.load, f32[1,8,128]{2,1,0:T(8,128)S(1)} %get-tuple-element.9.far, f32[8,128]{1,0:T(8,128)S(1)} %get-tuple-element.10.order), custom_call_target="tpu_custom_call" | custom-call | tf_op jit(solution)/shard_map/pallas_call | solution.py:535
